TPU v7x, 32 devices: a whole 2x2x4 slice. The times are simulated.
32 devices in a mesh: groups: 2 (over y), ctx: 4 (over z), tp: 4 (over x, core).
Axes of the slice: x: 2, y: 2, z: 4, core: 2. Of those that a mesh axis runs over, the one named last changes fastest.
Arguments:
- tokens: bfloat16 [2048, 4096], P(('groups', 'ctx', 'tp')), parts along dimension 0, may hold values from -6 to 6
- gain: float32 [4096], replicated, may hold values from 0.4 to 1.6
- wq: bfloat16 [4096, 4096], P('ctx', 'tp'), may hold values from -0.046875 to 0.046875
- wk: bfloat16 [4096, 1024], P('ctx', 'tp'), may hold values from -1.421875 to 1.421875
- wv: bfloat16 [4096, 1024], P('ctx', 'tp'), may hold values from -0.09375 to 0.09375
- wo: bfloat16 [4096, 4096], P('tp'), may hold values from -0.09375 to 0.09375
- sections: int32 [2048], P('groups'), parts along dimension 0, may hold values from 0 to 6, as said below
Outputs:
- attention_out: bfloat16 [2048, 4096], P(('groups', 'ctx', 'tp')), parts along dimension 0
There are 2 independent parts, one for each index of `groups`. A program takes and returns all parts, laid end to end along the dimension named above; an argument that names none is the same for every part. Nothing has to cross between parts.
Inputs may be any that keep to these rules, and one draw needn't show every extreme that they name: sections starts at 0, never falls, rises by at most 1 from one token to the next, and the last token has section 6.
All inputs are finite; a program needn't handle non-finite values.
Results may differ from a plain program's by a relative error of at most 0.01.
The roundings to bfloat16 on the way count: a program that leaves them out, or rounds other values in their place, can miss the bound.
Values may be sent and summed in bfloat16 or wider, within the bound.
A program may use at most 128 MiB of HBM per device.

v0:
```python
import math

import jax
import jax.numpy as jnp
from jax import lax
from jax.sharding import PartitionSpec as P

HD = 128


theta_base = 500000.0
eps_norm = 1e-05
neg_big = -1e30


def rotate(values, positions):
    half_dim = values.shape[-1] // 2
    freq = theta_base ** (-(jnp.arange(half_dim, dtype=jnp.float32) * 2.0 / values.shape[-1]))
    angle = positions.astype(jnp.float32)[:, None] * freq[None, :]
    cosine = jnp.cos(angle)[:, None, :]
    sine = jnp.sin(angle)[:, None, :]
    first = values[..., :half_dim]
    second = values[..., half_dim:]
    return jnp.concatenate(
        [first * cosine - second * sine, second * cosine + first * sine], axis=-1
    )


def norm_rows(tokens, gain):
    values = tokens.astype(jnp.float32)
    meansq = jnp.mean(values * values, axis=-1, keepdims=True)
    return (values * lax.rsqrt(meansq + eps_norm) * gain).astype(jnp.bfloat16)


def allowed(query_pos, query_section, key_pos, key_section):
    causal = key_pos[None, :] <= query_pos[:, None]
    same_example = key_section[None, :] // 3 == query_section[:, None] // 3
    visible = (key_section[None, :] % 3 == 0) | (key_section[None, :] == query_section[:, None])
    return causal & same_example & visible


def empty_carry(row_count, kv_count, group_size):
    running_max = jnp.full((row_count, kv_count, group_size), neg_big, jnp.float32)
    running_sum = jnp.zeros((row_count, kv_count, group_size), jnp.float32)
    accum = jnp.zeros((row_count, kv_count, group_size, HD), jnp.float32)
    return (running_max, running_sum, accum)


def absorb_range(carry, queries, query_pos, query_section, keys, vals, sections):
    key_count = keys.shape[0]
    block_len = math.gcd(key_count, 512)
    steps_count = key_count // block_len
    key_blocks = keys.reshape(steps_count, block_len, keys.shape[1], HD)
    value_blocks = vals.reshape(steps_count, block_len, vals.shape[1], HD)
    inv_root = 1.0 / math.sqrt(HD)

    def step(state, inputs):
        index_now, key_block, value_block = inputs
        first_key = index_now * block_len
        key_pos = first_key + jnp.arange(block_len, dtype=jnp.int32)
        key_section = lax.dynamic_slice_in_dim(sections, first_key, block_len)
        mask = allowed(query_pos, query_section, key_pos, key_section)[:, None, None, :]
        running_max, running_sum, accum = state
        scores = (
            jnp.einsum("rjgd,bjd->rjgb", queries, key_block, preferred_element_type=jnp.float32)
            * inv_root
        )
        scores = jnp.where(mask, scores, neg_big)
        new_max = jnp.maximum(running_max, jnp.max(scores, axis=-1))
        probs = jnp.where(mask, jnp.exp(scores - new_max[..., None]), 0.0)
        correction = jnp.exp(running_max - new_max)
        new_sum = running_sum * correction + jnp.sum(probs, axis=-1)
        mixed = jnp.einsum(
            "rjgb,bjd->rjgd",
            probs.astype(jnp.bfloat16),
            value_block,
            preferred_element_type=jnp.float32,
        )
        new_accum = accum * correction[..., None] + mixed
        return ((new_max, new_sum, new_accum), None)

    result, unused = lax.scan(
        step, carry, (jnp.arange(steps_count, dtype=jnp.int32), key_blocks, value_blocks)
    )
    return result


def finish(carry):
    running_max, running_sum, accum = carry
    row_count = accum.shape[0]
    return (accum / running_sum[..., None]).astype(jnp.bfloat16).reshape(row_count, -1)


def shards(tokens, gain, wq, wk, wv, wo, sections):
    row_count = tokens.shape[0]
    tp_count = lax.axis_size("tp")
    ctx_index = lax.axis_index("ctx")
    block_len = row_count * tp_count
    normalized = lax.all_gather(norm_rows(tokens, gain), "tp", axis=0, tiled=True)
    pieces = (
        lax.all_gather(wq, "ctx", axis=0, tiled=True),
        lax.all_gather(wk, "ctx", axis=0, tiled=True),
        lax.all_gather(wv, "ctx", axis=0, tiled=True),
    )
    query_acc, key_acc, value_acc = tuple(
        (
            jnp.dot(normalized, weight_piece, preferred_element_type=jnp.float32)
            for weight_piece in pieces
        )
    )
    head_count = wq.shape[1] // HD
    kv_count = wk.shape[1] // HD
    group_size = head_count // kv_count
    positions = ctx_index * block_len + jnp.arange(block_len, dtype=jnp.int32)
    queries = rotate(query_acc.reshape(block_len, head_count, HD), positions).astype(jnp.bfloat16)
    keys_local = rotate(key_acc.reshape(block_len, kv_count, HD), positions).astype(jnp.bfloat16)
    values_local = value_acc.astype(jnp.bfloat16).reshape(block_len, kv_count, HD)
    query_section = lax.dynamic_slice_in_dim(sections, ctx_index * block_len, block_len)
    grouped = queries.reshape(block_len, kv_count, group_size, HD)
    last_pos = ctx_index * block_len + block_len - 1
    pieces = (
        lax.all_gather(keys_local, "ctx", axis=0, tiled=True),
        lax.all_gather(values_local, "ctx", axis=0, tiled=True),
    )

    def attend(state):
        return absorb_range(
            state, grouped, positions, query_section, pieces[0], pieces[1], sections
        )

    def keep(state):
        return state

    carry = lax.cond(
        jnp.int32(0) <= last_pos, attend, keep, empty_carry(block_len, kv_count, group_size)
    )
    attended = finish(carry)
    return lax.psum_scatter(
        jnp.dot(attended, wo, preferred_element_type=jnp.float32).astype(jnp.bfloat16),
        "tp",
        scatter_dimension=0,
        tiled=True,
    )


def solution(mesh):
    placed = (
        P(("groups", "ctx", "tp"), None),
        P(),
        P("ctx", "tp"),
        P("ctx", "tp"),
        P("ctx", "tp"),
        P("tp", None),
        P("groups"),
    )
    return jax.shard_map(
        shards,
        mesh=mesh,
        in_specs=placed,
        out_specs=P(("groups", "ctx", "tp"), None),
        check_vma=False,
    )
```

profile of v0, /device:TPU:27, one launch (start us, length us, event | category | flops | bytes accessed | tf_op | source)
XLA Modules:
  0.0 362.9 jit_solution(3391649731179196666)
XLA Ops:
  6.5 0.0 all-gather.5.cloned.1.call-start
  6.5 1.2 fusion.25
  7.8 2.0 fusion.27
  9.8 0.0 all-gather.5.cloned.1.call-update
  9.9 0.0 all-gather.7.cloned.1.call-start
  9.9 0.7 all-gather.7.cloned.1.call-update
  10.6 0.0 all-gather.9.cloned.1.call-start
  10.7 0.7 all-gather.9.cloned.1.call-update
  11.3 0.0 all-gather.11.cloned.1.call-start
  11.4 0.5 all-gather.11.cloned.1.call-update
  11.9 0.0 reduce-scatter.2.cloned.1.call-start
  12.0 0.5 multiply_cosine_fusion
  12.5 20.5 %all-gather.5.cloned.1.call-done = bf16[256,4096]{1,0:T(8,128)(2,1)} async-done(((bf16[64,4096]{1,0:T(8,128)(2,1)}), bf16[256,4096]{1,0:T(8,128)(2,1)}) %all-gather.5.cloned.1.call-update) | async-done | bytes 2097168 | tf_op jit(solution)/shard_map/all_gather | solution.py:99
  33.0 0.0 copy-start.1
  33.0 46.1 %all-gather.7.cloned.1.call-done = bf16[4096,256]{1,0:T(8,128)(2,1)} async-done(((bf16[1024,256]{1,0:T(8,128)(2,1)}), bf16[4096,256]{1,0:T(8,128)(2,1)}) %all-gather.7.cloned.1.call-update) | async-done | bytes 2097168 | tf_op jit(solution)/shard_map/all_gather | solution.py:102
  79.1 3.1 fusion.30
  82.3 0.1 copy.28
  82.4 0.1 copy.29
  82.6 42.8 %all-gather.9.cloned.1.call-done = bf16[4096,256]{1,0:T(8,128)(2,1)} async-done(((bf16[1024,256]{1,0:T(8,128)(2,1)}), bf16[4096,256]{1,0:T(8,128)(2,1)}) %all-gather.9.cloned.1.call-update) | async-done | bytes 2097168 | tf_op jit(solution)/shard_map/all_gather | solution.py:103
  125.4 0.0 copy-done.1
  125.4 2.5 convolution_convert_fusion.1
  127.9 0.1 copy.20
  128.0 0.1 subtract_convert_fusion.1
  128.1 0.1 pad_maximum_fusion.1
  128.2 16.1 %all_gather.20 = bf16[1024,2,128]{2,0,1:T(8,128)(2,1)S(1)} all-gather(bf16[256,2,128]{2,0,1:T(8,128)(2,1)S(1)} %pad_maximum_fusion.1), channel_id=1, replica_groups=mesh['groups'=2,'ctx'=4,'tp'=4] {'ctx'}, dimensions={0}, use_global_device_ids=true | all-gather | bytes 655360 | tf_op jit(solution)/shard_map/all_gather | solution.py:122
  144.4 20.7 %all_gather.22 = bf16[1024,2,128]{2,0,1:T(8,128)(2,1)S(1)} all-gather(bf16[256,2,128]{2,0,1:T(8,128)(2,1)S(1)} %copy.20), channel_id=1, replica_groups=mesh['groups'=2,'ctx'=4,'tp'=4] {'ctx'}, dimensions={0}, use_global_device_ids=true | all-gather | bytes 655360 | tf_op jit(solution)/shard_map/all_gather | solution.py:123
  165.0 121.1 %all-gather.11.cloned.1.call-done = bf16[4096,1024]{1,0:T(8,128)(2,1)} async-done(((bf16[1024,1024]{1,0:T(8,128)(2,1)}), bf16[4096,1024]{1,0:T(8,128)(2,1)}) %all-gather.11.cloned.1.call-update) | async-done | bytes 8388624 | tf_op jit(solution)/shard_map/all_gather | solution.py:101
  286.2 5.7 %convolution_bitcast_fusion = f32[32,8,8,128]{3,1,2,0:T(8,128)S(1)} fusion(bf16[256,4096]{1,0:T(8,128)(2,1)S(1)} %copy-done.1, bf16[4096,1024]{1,0:T(8,128)(2,1)} %all-gather.11.cloned.1.call-done), kind=kOutput, calls=%fused_computation.36 | convolution fusion | flops 2147483648 | bytes 11534336 | tf_op jit(solution)/shard_map/dot_general | solution.py:107
  291.9 0.0 copy-start.2
  291.9 0.2 copy.30
  292.1 0.5 subtract_convert_fusion
  292.6 0.1 copy.21
  292.7 0.1 copy.22
  292.8 0.3 pad_maximum_fusion
  293.1 0.0 copy-done.2
  293.1 23.5 %conditional.1 = (f32[256,2,4]{0,2,1:T(4,128)}, f32[256,2,4,128]{0,3,2,1:T(8,128)}) conditional(s32[]{:T(128)} %convert_element_type.36, () %tuple.32, (bf16[1024,2,128]{2,0,1:T(8,128)(2,1)S(1)}, bf16[1024,2,128]{2,0,1:T(8,128)(2,1)S(1)}, s32[]{:T(128)}, s32[256]{0:T(256)S(1)}, s32[1024]{0:T(1024)S(1)}, ...), branch_computations={%region_1.0_spmd, %region_2.7_spmd} | conditional | flops 552096000 | bytes 33190862 | solution.py:134
  293.1 0.1 fusion.28
  293.2 23.4 %while.20 = (s32[]{:T(128)}, f32[256,2,4]{0,2,1:T(4,128)S(1)}, f32[256,2,4]{0,2,1:T(4,128)}, f32[256,2,4,128]{0,3,2,1:T(8,128)}, s32[2]{0:T(128)S(1)}, /*index=5...) while((s32[]{:T(128)}, f32[256,2,4]{0,2,1:T(4,128)S(1)}, ...), condition=%wide.region_6.6_spmd.clone, body=%wide.region_3.5_spmd.clone.sunk | while | flops 552095488 | bytes 33185540 | solution.py:82
  293.2 0.6 dynamic_slice.58
  294.4 0.1 fusion.51
  294.6 0.3 or_and_fusion.2
  294.9 2.7 fusion.52
  297.7 0.0 copy-start
  297.7 3.3 fusion.53
  301.0 0.6 fusion.54
  301.6 0.0 copy-done
  301.7 2.2 fusion.55
  303.9 0.6 dynamic_slice.58
  305.2 0.1 fusion.51
  305.3 0.3 or_and_fusion.2
  305.7 2.7 fusion.52
  308.4 0.0 copy-start
  308.4 3.3 fusion.53
  311.8 1.3 fusion.54
  313.1 0.0 copy-done
  313.1 3.5 fusion.55
  316.5 1.3 divide_convert_fusion
  317.9 7.1 %convolution_convert_fusion = bf16[256,4096]{1,0:T(8,128)(2,1)} fusion(bf16[256,1024]{0,1:T(8,128)(2,1)S(1)} %bitcast.75, bf16[1024,4096]{1,0:T(8,128)(2,1)} %param.16), kind=kOutput, calls=%fused_computation.35 | convolution fusion | flops 2148532224 | bytes 11010048 | tf_op jit(solution)/shard_map/dot_general | solution.py:139
  325.0 0.0 reduce-scatter.2.cloned.1.call-update
  325.0 31.4 %reduce-scatter.2.cloned.1.call-done = bf16[64,4096]{1,0:T(8,128)(2,1)} async-done(((bf16[256,4096]{1,0:T(8,128)(2,1)}), bf16[64,4096]{1,0:T(8,128)(2,1)}) %reduce-scatter.2.cloned.1.call-update) | async-done | bytes 524304 | tf_op jit(solution)/shard_map/reduce_scatter | solution.py:138
  (19 shorter events, 0.2 us)
Async XLA Ops:
  6.5 26.5 %all-gather.5.cloned.1.call-start = ((), (), s32[]{:S(2)}) async-start(), calls=%async_computation.1 | async-start | bytes 2621440 | tf_op jit(solution)/shard_map/all_gather | solution.py:99
  9.9 69.3 %all-gather.7.cloned.1.call-start = ((), (), s32[]{:S(2)}) async-start(), calls=%async_computation.2 | async-start | bytes 2621440 | tf_op jit(solution)/shard_map/all_gather | solution.py:102
  10.6 114.8 %all-gather.9.cloned.1.call-start = ((), (), s32[]{:S(2)}) async-start(), calls=%async_computation.3 | async-start | bytes 2621440 | tf_op jit(solution)/shard_map/all_gather | solution.py:103
  11.3 274.8 %all-gather.11.cloned.1.call-start = ((), (), s32[]{:S(2)}) async-start(), calls=%async_computation.4 | async-start | bytes 10485760 | tf_op jit(solution)/shard_map/all_gather | solution.py:101
  11.9 344.4 %reduce-scatter.2.cloned.1.call-start = ((), (), s32[]{:S(2)}) async-start(), calls=%async_computation.5 | async-start | bytes 2621440 | tf_op jit(solution)/shard_map/reduce_scatter | solution.py:138
  33.0 92.3 %copy-start.1 = (bf16[256,4096]{1,0:T(8,128)(2,1)S(1)}, bf16[256,4096]{1,0:T(8,128)(2,1)}, u32[]{:S(2)}) copy-start(bf16[256,4096]{1,0:T(8,128)(2,1)} %all-gather.5.cloned.1.call-done) | copy-start | bytes 6291460
  291.9 1.2 copy-start.2
  297.7 4.0 %copy-start = (f32[2,512,256,4]{2,1,3,0:T(8,128)S(1)}, f32[2,512,256,4]{2,1,3,0:T(8,128)}, u32[]{:S(2)}) copy-start(f32[2,512,256,4]{2,1,3,0:T(8,128)} %get-tuple-element.425) | copy-start | bytes 12582916 | tf_op jit(solution)/shard_map/cond/branch_1_fun/while
  308.4 4.7 %copy-start = (f32[2,512,256,4]{2,1,3,0:T(8,128)S(1)}, f32[2,512,256,4]{2,1,3,0:T(8,128)}, u32[]{:S(2)}) copy-start(f32[2,512,256,4]{2,1,3,0:T(8,128)} %get-tuple-element.425) | copy-start | bytes 12582916 | tf_op jit(solution)/shard_map/cond/branch_1_fun/while
Sparse Core Ops, SparseCore 0:
  10.0 23.0 all-gather.4
  34.6 44.4 all-gather.6
  80.7 44.6 all-gather.8
  126.8 159.3 all-gather.10
  325.1 31.1 reduce-scatter.1
where the time goes:
time: 366 us; the launch traced here: 363 us
  waiting for transfers between devices  264 us (72%)
  blocking collectives  36.8 us (10%)
  matrix products  29.6 us (8%)
  other arithmetic  15.8 us (4%)
  between operations  13.3 us (4%)
    all_gather x1, waiting for transfers between devices, shards(): lax.all_gather(wq, 'ctx', axis=0, tiled=True)  121 us
    all_gather x1, waiting for transfers between devices, shards(): lax.all_gather(wk, 'ctx', axis=0, tiled=True)  46.1 us
    all_gather x1, waiting for transfers between devices, shards(): lax.all_gather(wv, 'ctx', axis=0, tiled=True)  42.8 us
    reduce_scatter x1, waiting for transfers between devices, shards(): lax.psum_scatter(jnp.dot(attended, wo, preferred_element_type=jnp.float32...  31.4 us
    all_gather x1, blocking collectives, shards(): lax.all_gather(values_local, 'ctx', axis=0, tiled=True)  20.7 us
    all_gather x1, waiting for transfers between devices, shards(): lax.all_gather(norm_rows(tokens, gain), 'tp', axis=0, tiled=True)  20.5 us
    all_gather x1, blocking collectives, shards(): lax.all_gather(keys_local, 'ctx', axis=0, tiled=True)  16.1 us
    dot_general x3, matrix products, shards(): jnp.dot(normalized, weight_piece, preferred_element_type=jnp.float32)  11.4 us
  transfers between devices with their start and end apart: 5, of which 5 were waited for; matrix products, arithmetic and copies ran while one was open for 2% of the time, Pallas kernels for 0%

commit v1 on v0

v1 whole, which is shorter than its diff:
```python
import functools
import math

import jax
import jax.numpy as jnp
from jax import lax
from jax.experimental import pallas as pl
from jax.experimental.pallas import tpu as pltpu
from jax.sharding import PartitionSpec as P

HD = 128
MESH = pl.DeviceIdType.MESH
BF = jnp.bfloat16
F32 = jnp.float32

theta_base = 500000.0
eps_norm = 1e-05
neg_big = -1e30


def kernel(
    G, C, T, parts, chunks,
    tok, gain, cos, sin, secq, seck, wq, wk, wv, wo,
    out,
    nf, Wq, Wk, Wv, Wo, Kf, Vf, qbuf, att, term, pair, sib, xin,
    lsem, zsend, zrecv, ysend, yrecv, nsend, nrecv, ksend, krecv,
    s1send, s1recv, s2send, s2recv,
):
    g = lax.axis_index("groups")
    c = lax.axis_index("ctx")
    t = lax.axis_index("tp")
    X = T // 2
    x = t // 2
    core = lax.rem(t, 2)
    R, D = tok.shape
    B = R * T
    Kc, Nq = wq.shape
    Nk = wk.shape[1]
    kv = Nk // HD
    grp = Nq // Nk
    Kh = Kc // G
    part = Nq // parts
    total = seck.shape[1]
    inv_root = 1.0 / math.sqrt(HD)
    has_right = c < C - 1
    has_left = c > 0

    own = pl.ds(pl.multiple_of(c * Kc, Kc), Kc)
    loads = [
        pltpu.make_async_copy(wk, Wk.at[own], lsem.at[0]),
        pltpu.make_async_copy(wv, Wv.at[own], lsem.at[1]),
        pltpu.make_async_copy(wq, Wq.at[own], lsem.at[2]),
        pltpu.make_async_copy(wo, Wo, lsem.at[3]),
    ]
    for load in loads:
        load.start()

    barrier = pltpu.get_barrier_semaphore()

    @pl.when(has_right)
    def _():
        pl.semaphore_signal(barrier, inc=1, device_id={"ctx": c + 1}, device_id_type=MESH)

    @pl.when(has_left)
    def _():
        pl.semaphore_signal(barrier, inc=1, device_id={"ctx": c - 1}, device_id_type=MESH)

    for i in range(1, G):
        pl.semaphore_signal(
            barrier, inc=1, device_id={"groups": lax.rem(g + i, G)}, device_id_type=MESH
        )
    for i in range(1, T):
        pl.semaphore_signal(
            barrier, inc=1, device_id={"tp": lax.rem(t + i, T)}, device_id_type=MESH
        )
    pl.semaphore_wait(
        barrier, G - 1 + T - 1 + has_right.astype(jnp.int32) + has_left.astype(jnp.int32)
    )

    def piece(a, block, half):
        rows = pl.ds(pl.multiple_of(block * Kc + half * Kh, Kh), Kh)
        if a == 0:
            return Wk.at[rows]
        if a == 1:
            return Wv.at[rows]
        return Wq.at[rows, pl.ds((a - 2) * part, part)]

    def z_copy(a, block, right):
        ref = piece(a, block, g)
        return pltpu.make_async_remote_copy(
            src_ref=ref, dst_ref=ref,
            send_sem=zsend.at[a, block, right], recv_sem=zrecv.at[a, block],
            device_id={"ctx": c + 1 if right else c - 1}, device_id_type=MESH,
        )

    def y_copy(a, block, i, half):
        ref = piece(a, block, half)
        return pltpu.make_async_remote_copy(
            src_ref=ref, dst_ref=ref,
            send_sem=ysend.at[a, block, i], recv_sem=yrecv.at[a, block, i],
            device_id={"groups": lax.rem(g + i, G)}, device_id_type=MESH,
        )

    def send_own(a):
        @pl.when(has_right)
        def _():
            z_copy(a, c, 1).start()

        @pl.when(has_left)
        def _():
            z_copy(a, c, 0).start()

    def arrive(pieces, first, last):
        def body(s, carry):
            left = c - 1 - s
            right = c + 1 + s
            for a in pieces:
                @pl.when(left >= 0)
                def _():
                    z_copy(a, left, 1).wait_recv()

                    @pl.when(has_right)
                    def _():
                        z_copy(a, left, 1).start()

                    for i in range(1, G):
                        y_copy(a, left, i, g).start()

                @pl.when(right < C)
                def _():
                    z_copy(a, right, 0).wait_recv()

                    @pl.when(has_left)
                    def _():
                        z_copy(a, right, 0).start()

                    for i in range(1, G):
                        y_copy(a, right, i, g).start()
            return carry

        lax.fori_loop(first, last, body, 0)

    def y_wait(pieces):
        def body(block, carry):
            @pl.when(block != c)
            def _():
                for a in pieces:
                    for i in range(1, G):
                        y_copy(a, block, i, lax.rem(g + G - i, G)).wait_recv()
            return carry

        lax.fori_loop(0, C, body, 0)

    loads[0].wait()
    loads[1].wait()
    send_own(0)
    send_own(1)
    loads[2].wait()
    send_own(2)

    def n_copy(i, who):
        ref = nf.at[pl.ds(pl.multiple_of(who * R, R), R)]
        return pltpu.make_async_remote_copy(
            src_ref=ref, dst_ref=ref, send_sem=nsend.at[i], recv_sem=nrecv.at[i],
            device_id={"tp": lax.rem(t + i, T)}, device_id_type=MESH,
        )

    values = tok[...].astype(F32)
    meansq = jnp.mean(values * values, axis=-1, keepdims=True)
    nf[pl.ds(pl.multiple_of(t * R, R), R), :] = (
        values * lax.rsqrt(meansq + eps_norm) * gain[...]
    ).astype(BF)
    for i in range(1, T):
        n_copy(i, t).start()

    arrive((0, 1), 0, C - 1)
    for j in range(1, parts):
        send_own(2 + j)
    for i in range(1, T):
        n_copy(i, lax.rem(t + T - i, T)).wait_recv()

    def rotated(head):
        a = head[:, : HD // 2]
        b = head[:, HD // 2 :]
        cs = cos[...]
        sn = sin[...]
        return jnp.concatenate([a * cs - b * sn, b * cs + a * sn], axis=-1).astype(BF)

    def kv_rows(block):
        return pl.ds(pl.multiple_of(block * B, B), B)

    def kv_copy(which, block):
        ref = (Kf, Vf)[which].at[kv_rows(block)]
        return pltpu.make_async_remote_copy(
            src_ref=ref, dst_ref=ref,
            send_sem=ksend.at[which, block], recv_sem=krecv.at[which, block],
            device_id={"ctx": c + 1}, device_id_type=MESH,
        )

    y_wait((0, 1))
    raw = jnp.dot(nf[...], Wk[...], preferred_element_type=F32)
    for j in range(kv):
        Kf[kv_rows(c), j * HD : (j + 1) * HD] = rotated(raw[:, j * HD : (j + 1) * HD])
    Vf[kv_rows(c), :] = jnp.dot(nf[...], Wv[...], preferred_element_type=F32).astype(BF)

    @pl.when(has_right)
    def _():
        kv_copy(0, c).start()
        kv_copy(1, c).start()

    def blank(block, carry):
        Kf[kv_rows(block), :] = jnp.zeros((B, Nk), BF)
        Vf[kv_rows(block), :] = jnp.zeros((B, Nk), BF)
        return carry

    lax.fori_loop(c + 1, C, blank, 0)

    arrive((2,), 0, C - 1)

    def kv_arrive(s, carry):
        left = c - 1 - s

        @pl.when(left >= 0)
        def _():
            for which in range(2):
                kv_copy(which, left).wait_recv()

                @pl.when(has_right)
                def _():
                    kv_copy(which, left).start()
        return carry

    lax.fori_loop(0, C - 1, kv_arrive, 0)

    rows_now = max(16, min(B, (256 * 1024) // total))

    def attend(j):
        y_wait((2 + j,))
        raw = jnp.dot(
            nf[...], Wq[:, j * part : (j + 1) * part], preferred_element_type=F32
        )
        for h in range(part // HD):
            qbuf[h, :, :] = rotated(raw[:, h * HD : (h + 1) * HD])
        for h in range(part // HD):
            head = j * (part // HD) + h
            cols = slice((head // grp) * HD, (head // grp + 1) * HD)

            def tile(n, carry):
                rows = pl.ds(pl.multiple_of(n * rows_now, rows_now), rows_now)
                scores = (
                    lax.dot_general(
                        qbuf[h, rows, :], Kf[:, cols], (((1,), (1,)), ((), ())),
                        preferred_element_type=F32,
                    )
                    * inv_root
                )
                pos = c * B + n * rows_now + lax.broadcasted_iota(jnp.int32, (rows_now, total), 0)
                kpos = lax.broadcasted_iota(jnp.int32, (rows_now, total), 1)
                sq = secq[rows, :]
                sk = seck[...]
                third_q = (sq >= 3).astype(jnp.int32) + (sq >= 6).astype(jnp.int32)
                third_k = (sk >= 3).astype(jnp.int32) + (sk >= 6).astype(jnp.int32)
                prompt = sk == third_k * 3
                mask = (kpos <= pos) & (third_k == third_q) & (prompt | (sk == sq))
                scores = jnp.where(mask, scores, neg_big)
                top = jnp.max(scores, axis=-1, keepdims=True)
                weights = jnp.exp(scores - top)
                denom = jnp.sum(weights, axis=-1, keepdims=True)
                mixed = jnp.dot(weights.astype(BF), Vf[:, cols], preferred_element_type=F32)
                att[rows, head * HD : (head + 1) * HD] = (mixed / denom).astype(BF)
                return carry

            if rows_now == B:
                tile(0, 0)
            else:
                lax.fori_loop(0, B // rows_now, tile, 0)

    for j in range(parts):
        if j + 1 < parts:
            arrive((3 + j,), 0, 1)
        attend(j)
        if j + 1 < parts:
            arrive((3 + j,), 1, C - 1)

    loads[3].wait()
    width = D // chunks

    def t_rows(who):
        return pl.ds(pl.multiple_of(who * R, R), R)

    def cols_of(n):
        return pl.ds(n * width, width)

    def s1_copy(n, xi):
        return pltpu.make_async_remote_copy(
            src_ref=term.at[t_rows(xi * 2 + 1 - core), cols_of(n)],
            dst_ref=sib.at[xi, :, cols_of(n)],
            send_sem=s1send.at[n, xi], recv_sem=s1recv.at[n, xi],
            device_id={"tp": x * 2 + 1 - core}, device_id_type=MESH,
        )

    def s2_copy(n, i, source):
        return pltpu.make_async_remote_copy(
            src_ref=pair.at[i - 1, :, cols_of(n)],
            dst_ref=xin.at[i - 1, :, cols_of(n)],
            send_sem=s2send.at[n, i], recv_sem=s2recv.at[n, i],
            device_id={"tp": lax.rem(x + i, X) * 2 + core}, device_id_type=MESH,
        )

    def project(n):
        term[:, cols_of(n)] = jnp.dot(
            att[...], Wo[:, cols_of(n)], preferred_element_type=F32
        ).astype(BF)
        for xi in range(X):
            s1_copy(n, xi).start()

    def pass_on(n):
        for xi in range(X):
            s1_copy(n, xi).wait_recv()
        for i in range(1, X):
            there = lax.rem(x + i, X)
            pair[i - 1, :, cols_of(n)] = (
                term[t_rows(there * 2 + core), cols_of(n)].astype(F32)
                + sib[there, :, cols_of(n)].astype(F32)
            ).astype(BF)
            s2_copy(n, i, there).start()

    for n in range(chunks):
        project(n)
        if n:
            pass_on(n - 1)
    pass_on(chunks - 1)
    for n in range(chunks):
        total_now = term[t_rows(t), cols_of(n)].astype(F32) + sib[x, :, cols_of(n)].astype(F32)
        for i in range(1, X):
            s2_copy(n, i, x).wait_recv()
            total_now = total_now + xin[i - 1, :, cols_of(n)].astype(F32)
        out[:, cols_of(n)] = total_now.astype(BF)

    for n in range(chunks):
        for xi in range(X):
            s1_copy(n, xi).wait_send()
        for i in range(1, X):
            s2_copy(n, i, x).wait_send()
    for i in range(1, T):
        n_copy(i, t).wait_send()

    def drain(block, carry):
        for a in range(2 + parts):
            @pl.when((block <= c) & has_right)
            def _():
                z_copy(a, block, 1).wait_send()

            @pl.when((block >= c) & has_left)
            def _():
                z_copy(a, block, 0).wait_send()

            @pl.when(block != c)
            def _():
                for i in range(1, G):
                    y_copy(a, block, i, g).wait_send()

        @pl.when((block <= c) & has_right)
        def _():
            kv_copy(0, block).wait_send()
            kv_copy(1, block).wait_send()
        return carry

    lax.fori_loop(0, C, drain, 0)


def shards(G, C, T, tokens, gain, wq, wk, wv, wo, sections):
    R, D = tokens.shape
    B = R * T
    Kc, Nq = wq.shape
    Nk = wk.shape[1]
    K = Kc * C
    kv = Nk // HD
    parts = kv
    part = Nq // parts
    chunks = 4
    X = T // 2
    total = sections.shape[0]
    A = 2 + parts
    c = lax.axis_index("ctx")
    positions = c * B + jnp.arange(B, dtype=jnp.int32)
    freq = theta_base ** (-(jnp.arange(HD // 2, dtype=F32) * 2.0 / HD))
    angle = positions.astype(F32)[:, None] * freq[None, :]
    secq = lax.dynamic_slice_in_dim(sections, c * B, B)[:, None]
    vm = pl.BlockSpec(memory_space=pltpu.VMEM)
    hbm = pl.BlockSpec(memory_space=pltpu.HBM)
    dma = pltpu.SemaphoreType.DMA
    return pl.pallas_call(
        functools.partial(kernel, G, C, T, parts, chunks),
        out_shape=jax.ShapeDtypeStruct((R, D), BF),
        in_specs=[vm] * 6 + [hbm] * 4,
        out_specs=vm,
        scratch_shapes=[
            pltpu.VMEM((B, D), BF),
            pltpu.VMEM((K, Nq), BF),
            pltpu.VMEM((K, Nk), BF),
            pltpu.VMEM((K, Nk), BF),
            pltpu.VMEM(wo.shape, BF),
            pltpu.VMEM((total, Nk), BF),
            pltpu.VMEM((total, Nk), BF),
            pltpu.VMEM((part // HD, B, HD), BF),
            pltpu.VMEM((B, Nq), BF),
            pltpu.VMEM((B, D), BF),
            pltpu.VMEM((X - 1, R, D), BF),
            pltpu.VMEM((X, R, D), BF),
            pltpu.VMEM((X - 1, R, D), BF),
            dma((4,)),
            dma((A, C, 2)),
            dma((A, C)),
            dma((A, C, G)),
            dma((A, C, G)),
            dma((T,)),
            dma((T,)),
            dma((2, C)),
            dma((2, C)),
            dma((chunks, X)),
            dma((chunks, X)),
            dma((chunks, X)),
            dma((chunks, X)),
        ],
        compiler_params=pltpu.CompilerParams(
            collective_id=0, has_side_effects=True, vmem_limit_bytes=60 * 1024 * 1024
        ),
    )(tokens, gain[None, :], jnp.cos(angle), jnp.sin(angle), secq, sections[None, :],
      wq, wk, wv, wo)


def solution(mesh):
    placed = (
        P(("groups", "ctx", "tp"), None),
        P(),
        P("ctx", "tp"),
        P("ctx", "tp"),
        P("ctx", "tp"),
        P("tp", None),
        P("groups"),
    )
    return jax.shard_map(
        functools.partial(shards, mesh.shape["groups"], mesh.shape["ctx"], mesh.shape["tp"]),
        mesh=mesh,
        in_specs=placed,
        out_specs=P(("groups", "ctx", "tp"), None),
        check_vma=False,
    )
```

time: 366 us -> 162 us (0.44)
  waiting for transfers between devices: 264 us -> 0 us
  Pallas kernels: 0 us -> 157 us
  blocking collectives: 36.8 us -> 0 us
  matrix products: 29.6 us -> 0 us
  other arithmetic: 15.8 us -> 1.25 us
  between operations: 13.3 us -> 0.01 us
    all_gather x4 -> x0, waiting for transfers between devices: 231 us -> none  [the longest x1 121 us: shards(): lax.all_gather(wq, 'ctx', axis=0, tiled=True)]
    pallas_call x0 -> x1, Pallas kernels: none -> 157 us  [shards(): pl.pallas_call(functools.partial(kernel, G, C, T, parts, chunks), out_sha...]
    all_gather x2 -> x0, blocking collectives: 36.8 us -> none  [the longest x1 20.7 us: shards(): lax.all_gather(values_local, 'ctx', axis=0, tiled=True)]
    reduce_scatter x1 -> x0, waiting for transfers between devices: 31.4 us -> none  [shards(): lax.psum_scatter(jnp.dot(attended, wo, preferred_element_type=jnp.float32...]
    dot_general x8 -> x0, matrix products: 29.6 us -> none  [the longest x3 11.4 us: shards(): jnp.dot(normalized, weight_piece, preferred_element_type=jnp.float32)]
    reduce_sum x3 -> x0, other arithmetic: 7.94 us -> none  [the longest x2 6.7 us: step(): new_sum = running_sum * correction + jnp.sum(probs, axis=-1)]
  transfers between devices with their start and end apart: 5 -> 0, of which waited for: 5 -> 0; matrix products, arithmetic and copies ran while one was open for 2% -> 0% of each run, Pallas kernels for 0% -> 0%
where the time goes in v1:
time: 162 us; the launch traced here: 161 us
  Pallas kernels  157 us (97%)
  local copies, waits for them, and re-layouts  3.43 us (2%)
    pallas_call x1, Pallas kernels, shards(): pl.pallas_call(functools.partial(kernel, G, C, T, parts, chunks), out_sha...  157 us

profile of v1, /device:TPU:27, one launch (start us, length us, event | category | flops | bytes accessed | tf_op | source)
XLA Modules:
  0.0 161.4 jit_solution(11279120153764489704)
XLA Ops:
  0.0 0.8 dynamic_slice.3
  0.8 0.8 copy.8.secq
  1.6 1.2 multiply_sine_fusion
  2.8 156.7 %shard_map.73 = bf16[64,4096]{1,0:T(8,128)(2,1)} custom-call(bf16[64,4096]{1,0:T(8,128)(2,1)} %tok.1, f32[1,4096]{1,0:T(1,128)} %bitcast.3, f32[256,64]{1,0:T(8,128)} %get-tuple-element.6.cos, f32[256,64]{1,0:T(8,128)} %get-tuple-element.5.sin, s32[256,1]{1,0:T(8,128)} %copy.8.secq, s32[1,1024]{1,0:T(1,128)} %bitcast.4, bf16[1024,1024]{1,0:T(8,128)(2,1)} %wq.1, ...), custom_call_target="tpu_custom_call" | custom-call | tf_op jit(solution)/shard_map/pallas_call | solution.py:393
  159.6 1.9 %copy.10 = bf16[64,4096]{1,0:T(8,128)(2,1)} copy(bf16[64,4096]{1,0:T(8,128)(2,1)} %shard_map.73) | data formatting | bytes 1048576
  (2 shorter events, 0.0 us)

commit v2 on v1

--- a/solution.py
+++ b/solution.py
@@ -22,8 +22,9 @@
     G, C, T, parts, chunks,
     tok, gain, cos, sin, secq, seck, wq, wk, wv, wo,
     out,
-    nf, Wq, Wk, Wv, Wo, Kf, Vf, qbuf, att, term, pair, sib, xin,
-    lsem, zsend, zrecv, ysend, yrecv, nsend, nrecv, ksend, krecv,
+    nf, xall, acc, Wq, Wk, Wv, Wo, Kf, Vf, qbuf, att, term, pair, sib, xin,
+    lsem, zsend, zrecv, ysend, yrecv, nsend, nrecv, x1send, x1recv, x2send, x2recv,
+    rsend, rrecv, ksend, krecv,
     s1send, s1recv, s2send, s2recv,
 ):
     g = lax.axis_index("groups")
@@ -49,7 +50,7 @@
     loads = [
         pltpu.make_async_copy(wk, Wk.at[own], lsem.at[0]),
         pltpu.make_async_copy(wv, Wv.at[own], lsem.at[1]),
-        pltpu.make_async_copy(wq, Wq.at[own], lsem.at[2]),
+        pltpu.make_async_copy(wq, Wq, lsem.at[2]),
         pltpu.make_async_copy(wo, Wo, lsem.at[3]),
     ]
     for load in loads:
@@ -57,14 +58,10 @@
 
     barrier = pltpu.get_barrier_semaphore()
 
-    @pl.when(has_right)
-    def _():
-        pl.semaphore_signal(barrier, inc=1, device_id={"ctx": c + 1}, device_id_type=MESH)
-
-    @pl.when(has_left)
-    def _():
-        pl.semaphore_signal(barrier, inc=1, device_id={"ctx": c - 1}, device_id_type=MESH)
-
+    for i in range(1, C):
+        pl.semaphore_signal(
+            barrier, inc=1, device_id={"ctx": lax.rem(c + i, C)}, device_id_type=MESH
+        )
     for i in range(1, G):
         pl.semaphore_signal(
             barrier, inc=1, device_id={"groups": lax.rem(g + i, G)}, device_id_type=MESH
@@ -73,17 +70,58 @@
         pl.semaphore_signal(
             barrier, inc=1, device_id={"tp": lax.rem(t + i, T)}, device_id_type=MESH
         )
-    pl.semaphore_wait(
-        barrier, G - 1 + T - 1 + has_right.astype(jnp.int32) + has_left.astype(jnp.int32)
-    )
+
+    def t_rows(who):
+        return pl.ds(pl.multiple_of(who * R, R), R)
+
+    values = tok[...].astype(F32)
+    meansq = jnp.mean(values * values, axis=-1, keepdims=True)
+    nf[t_rows(t), :] = (values * lax.rsqrt(meansq + eps_norm) * gain[...]).astype(BF)
+    pl.semaphore_wait(barrier, G - 1 + T - 1 + C - 1)
+
+    def feats(who):
+        return pl.ds(pl.multiple_of(who * Kc, Kc), Kc)
+
+    def x_rows(block, who):
+        return pl.ds(pl.multiple_of(block * B + who * R, R), R)
+
+    def x1_copy(target, source):
+        return pltpu.make_async_remote_copy(
+            src_ref=nf.at[t_rows(t), feats(target)], dst_ref=xall.at[x_rows(source, t)],
+            send_sem=x1send.at[target], recv_sem=x1recv.at[source],
+            device_id={"ctx": target}, device_id_type=MESH,
+        )
+
+    def x2_copy(block, i, who):
+        ref = xall.at[x_rows(block, who)]
+        return pltpu.make_async_remote_copy(
+            src_ref=ref, dst_ref=ref,
+            send_sem=x2send.at[block, i], recv_sem=x2recv.at[block, i],
+            device_id={"tp": lax.rem(t + i, T)}, device_id_type=MESH,
+        )
+
+    def farthest_first(act):
+        def body(n, carry):
+            far = C - 1 - n
+
+            @pl.when(c + far < C)
+            def _():
+                act(c + far)
+
+            @pl.when(c - far >= 0)
+            def _():
+                act(c - far)
+            return carry
+
+        lax.fori_loop(0, C - 1, body, 0)
+
+    farthest_first(lambda target: x1_copy(target, c).start())
 
     def piece(a, block, half):
         rows = pl.ds(pl.multiple_of(block * Kc + half * Kh, Kh), Kh)
         if a == 0:
             return Wk.at[rows]
-        if a == 1:
-            return Wv.at[rows]
-        return Wq.at[rows, pl.ds((a - 2) * part, part)]
+        return Wv.at[rows]
 
     def z_copy(a, block, right):
         ref = piece(a, block, g)
@@ -155,27 +193,88 @@
     loads[1].wait()
     send_own(0)
     send_own(1)
-    loads[2].wait()
-    send_own(2)
+
+    def share(block):
+        x1_copy(block, block).wait_recv()
+        for i in range(1, T):
+            x2_copy(block, i, t).start()
+
+    farthest_first(share)
 
     def n_copy(i, who):
-        ref = nf.at[pl.ds(pl.multiple_of(who * R, R), R)]
+        ref = nf.at[t_rows(who)]
         return pltpu.make_async_remote_copy(
             src_ref=ref, dst_ref=ref, send_sem=nsend.at[i], recv_sem=nrecv.at[i],
             device_id={"tp": lax.rem(t + i, T)}, device_id_type=MESH,
         )
 
-    values = tok[...].astype(F32)
-    meansq = jnp.mean(values * values, axis=-1, keepdims=True)
-    nf[pl.ds(pl.multiple_of(t * R, R), R), :] = (
-        values * lax.rsqrt(meansq + eps_norm) * gain[...]
-    ).astype(BF)
     for i in range(1, T):
         n_copy(i, t).start()
 
-    arrive((0, 1), 0, C - 1)
-    for j in range(1, parts):
-        send_own(2 + j)
+    @pl.when(c == 0)
+    def _():
+        acc[0, :, :, :] = jnp.zeros((parts, B, part), F32)
+
+    @pl.when(c == C - 1)
+    def _():
+        acc[C, :, :, :] = jnp.zeros((parts, B, part), F32)
+
+    loads[2].wait()
+
+    def q_copy(p, block, back):
+        nbr = c + 1 - 2 * back
+        slot = jnp.where((back == 1) & (nbr == block), C, block)
+        return pltpu.make_async_remote_copy(
+            src_ref=acc.at[block, p], dst_ref=acc.at[slot, p],
+            send_sem=rsend.at[p, block], recv_sem=rrecv.at[p, slot],
+            device_id={"ctx": nbr}, device_id_type=MESH,
+        )
+
+    def q_arrival(p, slot):
+        return pltpu.make_async_remote_copy(
+            src_ref=acc.at[slot, p], dst_ref=acc.at[slot, p],
+            send_sem=rsend.at[p, 0], recv_sem=rrecv.at[p, slot],
+            device_id={"ctx": c}, device_id_type=MESH,
+        )
+
+    def q_hop(p, k):
+        def way(n, carry):
+            back = jnp.where(2 * c >= C, 1 - n, n)
+            block = jnp.where(back == 1, k, C - 1 - k)
+            valid = jnp.where(back == 1, block < c, block > c)
+            incoming = jnp.where(back == 1, c < C - 1, c > 0)
+
+            @pl.when(valid)
+            def _():
+                if p == 0:
+                    for i in range(1, T):
+                        x2_copy(block, i, lax.rem(t + T - i, T)).wait_recv()
+                own_sum = jnp.dot(
+                    xall[pl.ds(pl.multiple_of(block * B, B), B), :],
+                    Wq[:, p * part : (p + 1) * part],
+                    preferred_element_type=F32,
+                )
+
+                @pl.when(incoming)
+                def _():
+                    q_arrival(p, block).wait_recv()
+                    acc[block, p, :, :] = acc[block, p, :, :] + own_sum
+
+                @pl.when(jnp.logical_not(incoming))
+                def _():
+                    acc[block, p, :, :] = own_sum
+
+                q_copy(p, block, back).start()
+            return carry
+
+        lax.fori_loop(0, 2, way, 0)
+
+    def first_round(k, carry):
+        q_hop(0, k)
+        arrive((0, 1), k, k + 1)
+        return carry
+
+    lax.fori_loop(0, C - 1, first_round, 0)
     for i in range(1, T):
         n_copy(i, lax.rem(t + T - i, T)).wait_recv()
 
@@ -215,9 +314,9 @@
 
     lax.fori_loop(c + 1, C, blank, 0)
 
-    arrive((2,), 0, C - 1)
-
-    def kv_arrive(s, carry):
+    def later_round(s, carry):
+        for p in range(1, parts):
+            q_hop(p, s)
         left = c - 1 - s
 
         @pl.when(left >= 0)
@@ -230,14 +329,23 @@
                     kv_copy(which, left).start()
         return carry
 
-    lax.fori_loop(0, C - 1, kv_arrive, 0)
+    lax.fori_loop(0, C - 1, later_round, 0)
 
     rows_now = max(16, min(B, (256 * 1024) // total))
 
     def attend(j):
-        y_wait((2 + j,))
-        raw = jnp.dot(
-            nf[...], Wq[:, j * part : (j + 1) * part], preferred_element_type=F32
+        @pl.when(has_left)
+        def _():
+            q_arrival(j, c).wait_recv()
+
+        @pl.when(has_right)
+        def _():
+            q_arrival(j, C).wait_recv()
+
+        raw = (
+            jnp.dot(nf[:, feats(c)], Wq[:, j * part : (j + 1) * part], preferred_element_type=F32)
+            + acc[c, j, :, :]
+            + acc[C, j, :, :]
         )
         for h in range(part // HD):
             qbuf[h, :, :] = rotated(raw[:, h * HD : (h + 1) * HD])
@@ -276,17 +384,10 @@
                 lax.fori_loop(0, B // rows_now, tile, 0)
 
     for j in range(parts):
-        if j + 1 < parts:
-            arrive((3 + j,), 0, 1)
         attend(j)
-        if j + 1 < parts:
-            arrive((3 + j,), 1, C - 1)
 
     loads[3].wait()
     width = D // chunks
-
-    def t_rows(who):
-        return pl.ds(pl.multiple_of(who * R, R), R)
 
     def cols_of(n):
         return pl.ds(n * width, width)
@@ -346,7 +447,7 @@
         n_copy(i, t).wait_send()
 
     def drain(block, carry):
-        for a in range(2 + parts):
+        for a in range(2):
             @pl.when((block <= c) & has_right)
             def _():
                 z_copy(a, block, 1).wait_send()
@@ -364,6 +465,14 @@
         def _():
             kv_copy(0, block).wait_send()
             kv_copy(1, block).wait_send()
+
+        @pl.when(block != c)
+        def _():
+            x1_copy(block, c).wait_send()
+            for i in range(1, T):
+                x2_copy(block, i, t).wait_send()
+            for p in range(parts):
+                q_copy(p, block, (block < c).astype(jnp.int32)).wait_send()
         return carry
 
     lax.fori_loop(0, C, drain, 0)
@@ -381,7 +490,7 @@
     chunks = 4
     X = T // 2
     total = sections.shape[0]
-    A = 2 + parts
+    A = 2
     c = lax.axis_index("ctx")
     positions = c * B + jnp.arange(B, dtype=jnp.int32)
     freq = theta_base ** (-(jnp.arange(HD // 2, dtype=F32) * 2.0 / HD))
@@ -397,7 +506,9 @@
         out_specs=vm,
         scratch_shapes=[
             pltpu.VMEM((B, D), BF),
-            pltpu.VMEM((K, Nq), BF),
+            pltpu.VMEM((total, Kc), BF),
+            pltpu.VMEM((C + 1, parts, B, part), F32),
+            pltpu.VMEM((Kc, Nq), BF),
             pltpu.VMEM((K, Nk), BF),
             pltpu.VMEM((K, Nk), BF),
             pltpu.VMEM(wo.shape, BF),
@@ -416,6 +527,12 @@
             dma((A, C, G)),
             dma((T,)),
             dma((T,)),
+            dma((C,)),
+            dma((C,)),
+            dma((C, T)),
+            dma((C, T)),
+            dma((parts, C)),
+            dma((parts, C + 1)),
             dma((2, C)),
             dma((2, C)),
             dma((chunks, X)),

time: 162 us -> 169 us (1.043); the launches traced: 161 us -> 166 us
  Pallas kernels: 157 us -> 161 us
    pallas_call x1, Pallas kernels: 157 us -> 161 us  [shards(): pl.pallas_call(functools.partial(kernel, G, C, T, parts, chunks), out_sha...]
where the time goes in v2:
time: 169 us; the launch traced here: 166 us
  Pallas kernels  161 us (95%)
  local copies, waits for them, and re-layouts  3.43 us (2%)
    pallas_call x1, Pallas kernels, shards(): pl.pallas_call(functools.partial(kernel, G, C, T, parts, chunks), out_sha...  161 us

profile of v2, /device:TPU:27, one launch (start us, length us, event | category | flops | bytes accessed | tf_op | source)
XLA Modules:
  0.0 166.2 jit_solution(1772796401447598419)
XLA Ops:
  0.0 0.8 dynamic_slice.3
  0.8 0.8 copy.8.secq
  1.6 1.2 multiply_sine_fusion
  2.8 161.5 %shard_map.73 = bf16[64,4096]{1,0:T(8,128)(2,1)} custom-call(bf16[64,4096]{1,0:T(8,128)(2,1)} %tok.1, f32[1,4096]{1,0:T(1,128)} %bitcast.3, f32[256,64]{1,0:T(8,128)} %get-tuple-element.6.cos, f32[256,64]{1,0:T(8,128)} %get-tuple-element.5.sin, s32[256,1]{1,0:T(8,128)} %copy.8.secq, s32[1,1024]{1,0:T(1,128)} %bitcast.4, bf16[1024,1024]{1,0:T(8,128)(2,1)} %wq.1, ...), custom_call_target="tpu_custom_call" | custom-call | tf_op jit(solution)/shard_map/pallas_call | solution.py:502
  164.3 1.9 %copy.10 = bf16[64,4096]{1,0:T(8,128)(2,1)} copy(bf16[64,4096]{1,0:T(8,128)(2,1)} %shard_map.73) | data formatting | bytes 1048576
  (2 shorter events, 0.0 us)

commit v3 on v2

--- a/solution.py
+++ b/solution.py
@@ -92,13 +92,43 @@
             device_id={"ctx": target}, device_id_type=MESH,
         )
 
-    def x2_copy(block, i, who):
+    sibling = x * 2 + 1 - core
+
+    def mate(i, k):
+        return lax.rem(x + i, X) * 2 + k
+
+    def x2_copy(block, slot, target, who):
         ref = xall.at[x_rows(block, who)]
         return pltpu.make_async_remote_copy(
             src_ref=ref, dst_ref=ref,
-            send_sem=x2send.at[block, i], recv_sem=x2recv.at[block, i],
-            device_id={"tp": lax.rem(t + i, T)}, device_id_type=MESH,
-        )
+            send_sem=x2send.at[block, slot], recv_sem=x2recv.at[block, who],
+            device_id={"tp": target}, device_id_type=MESH,
+        )
+
+    def n_copy(slot, target, who):
+        ref = nf.at[t_rows(who)]
+        return pltpu.make_async_remote_copy(
+            src_ref=ref, dst_ref=ref, send_sem=nsend.at[slot], recv_sem=nrecv.at[who],
+            device_id={"tp": target}, device_id_type=MESH,
+        )
+
+    def spread(copy):
+        for i in range(1, X):
+            copy(i, mate(i, core), t).start()
+        copy(0, sibling, t).start()
+
+    def spread_on(copy):
+        for i in range(1, X):
+            copy(0, sibling, mate(i, core)).wait_recv()
+            copy(X - 1 + i, sibling, mate(i, core)).start()
+
+    def spread_wait(copy):
+        for i in range(X):
+            copy(0, sibling, mate(i, 1 - core)).wait_recv()
+
+    def spread_drain(copy):
+        for i in range(2 * X - 1):
+            copy(i, sibling, t).wait_send()
 
     def farthest_first(act):
         def body(n, carry):
@@ -196,20 +226,11 @@
 
     def share(block):
         x1_copy(block, block).wait_recv()
-        for i in range(1, T):
-            x2_copy(block, i, t).start()
+        spread(functools.partial(x2_copy, block))
 
     farthest_first(share)
-
-    def n_copy(i, who):
-        ref = nf.at[t_rows(who)]
-        return pltpu.make_async_remote_copy(
-            src_ref=ref, dst_ref=ref, send_sem=nsend.at[i], recv_sem=nrecv.at[i],
-            device_id={"tp": lax.rem(t + i, T)}, device_id_type=MESH,
-        )
-
-    for i in range(1, T):
-        n_copy(i, t).start()
+    spread(n_copy)
+    farthest_first(lambda block: spread_on(functools.partial(x2_copy, block)))
 
     @pl.when(c == 0)
     def _():
@@ -247,8 +268,7 @@
             @pl.when(valid)
             def _():
                 if p == 0:
-                    for i in range(1, T):
-                        x2_copy(block, i, lax.rem(t + T - i, T)).wait_recv()
+                    spread_wait(functools.partial(x2_copy, block))
                 own_sum = jnp.dot(
                     xall[pl.ds(pl.multiple_of(block * B, B), B), :],
                     Wq[:, p * part : (p + 1) * part],
@@ -269,14 +289,34 @@
 
         lax.fori_loop(0, 2, way, 0)
 
-    def first_round(k, carry):
-        q_hop(0, k)
-        arrive((0, 1), k, k + 1)
+    is_end = jnp.logical_or(c == 0, c == C - 1)
+    early = max(C - 2, 1)
+
+    def hops(p, first, last):
+        def body(k, carry):
+            q_hop(p, k)
+            return carry
+
+        lax.fori_loop(first, last, body, 0)
+
+    def phase(n, carry):
+        @pl.when(is_end == (n == 0))
+        def _():
+            hops(0, 0, C - 1)
+
+            @pl.when(is_end)
+            def _():
+                for p in range(1, parts):
+                    hops(p, 0, early)
+
+        @pl.when(n == 0)
+        def _():
+            arrive((0, 1), 0, C - 1)
         return carry
 
-    lax.fori_loop(0, C - 1, first_round, 0)
-    for i in range(1, T):
-        n_copy(i, lax.rem(t + T - i, T)).wait_recv()
+    lax.fori_loop(0, 2, phase, 0)
+    spread_on(n_copy)
+    spread_wait(n_copy)
 
     def rotated(head):
         a = head[:, : HD // 2]
@@ -316,7 +356,9 @@
 
     def later_round(s, carry):
         for p in range(1, parts):
-            q_hop(p, s)
+            @pl.when(jnp.logical_not(is_end) | (s >= early))
+            def _():
+                q_hop(p, s)
         left = c - 1 - s
 
         @pl.when(left >= 0)
@@ -443,8 +485,7 @@
             s1_copy(n, xi).wait_send()
         for i in range(1, X):
             s2_copy(n, i, x).wait_send()
-    for i in range(1, T):
-        n_copy(i, t).wait_send()
+    spread_drain(n_copy)
 
     def drain(block, carry):
         for a in range(2):
@@ -469,8 +510,7 @@
         @pl.when(block != c)
         def _():
             x1_copy(block, c).wait_send()
-            for i in range(1, T):
-                x2_copy(block, i, t).wait_send()
+            spread_drain(functools.partial(x2_copy, block))
             for p in range(parts):
                 q_copy(p, block, (block < c).astype(jnp.int32)).wait_send()
         return carry

time: 169 us -> 136 us (0.80)
  the two profiles are of different devices: /device:TPU:27 before, /device:TPU:17 now
where the time goes in v3:
time: 136 us
  Pallas kernels  131 us (96%)
  local copies, waits for them, and re-layouts  3.43 us (3%)
    pallas_call x1, Pallas kernels, shards(): pl.pallas_call(functools.partial(kernel, G, C, T, parts, chunks), out_sha...  131 us

profile of v3, /device:TPU:17, one launch (start us, length us, event | category | flops | bytes accessed | tf_op | source)
XLA Modules:
  0.0 135.9 jit_solution(12580707733109234829)
XLA Ops:
  0.0 0.8 dynamic_slice.3
  0.8 0.8 copy.8.secq
  1.6 1.2 multiply_sine_fusion
  2.8 131.2 %shard_map.73 = bf16[64,4096]{1,0:T(8,128)(2,1)} custom-call(bf16[64,4096]{1,0:T(8,128)(2,1)} %tok.1, f32[1,4096]{1,0:T(1,128)} %bitcast.3, f32[256,64]{1,0:T(8,128)} %get-tuple-element.6.cos, f32[256,64]{1,0:T(8,128)} %get-tuple-element.5.sin, s32[256,1]{1,0:T(8,128)} %copy.8.secq, s32[1,1024]{1,0:T(1,128)} %bitcast.4, bf16[1024,1024]{1,0:T(8,128)(2,1)} %wq.1, ...), custom_call_target="tpu_custom_call" | custom-call | tf_op jit(solution)/shard_map/pallas_call | solution.py:542
  134.0 1.9 %copy.10 = bf16[64,4096]{1,0:T(8,128)(2,1)} copy(bf16[64,4096]{1,0:T(8,128)(2,1)} %shard_map.73) | data formatting | bytes 1048576
  (2 shorter events, 0.0 us)
